TPU v7x, 256 devices: a whole 4x4x8 slice. The times are simulated.
256 devices in a mesh: dom: 64 (over z, y, core), rep: 4 (over x).
Axes of the slice: x: 4, y: 4, z: 8, core: 2. Of those that a mesh axis runs over, the one named last changes fastest.
Arguments:
- features: bfloat16 [65536, 512], P('dom', 'rep'), may hold values from -6 to 6
- weight: bfloat16 [512, 512], P(None, 'rep'), may hold values from -0.25 to 0.25
- bias: bfloat16 [512], P('rep'), may hold values from -3 to 3
- cotangent: bfloat16 [65536, 512], P('dom', 'rep'), may hold values from -6 to 6
- tile_vals: bfloat16 [64, 160, 128, 128], P('dom'), may hold values from -0.21875 to 0.21875
- tile_row: int32 [64, 160], P('dom'), may hold values from 0 to 8, as said below
- tile_src: int32 [64, 160], P('dom'), may hold values from 0 to 135, as said below
- send_blocks: int32 [64, 64, 2], P('dom'), may hold values from 0 to 7
- send_count: int32 [64, 64], P('dom'), may hold values from 0 to 2, as said below
Outputs:
- out: bfloat16 [65536, 512], P('dom', 'rep')
- grad_input: bfloat16 [65536, 512], P('dom', 'rep')
- grad_weight: float32 [512, 512], P(None, 'rep')
- grad_bias: float32 [512], P('rep')
Inputs may be any that keep to these rules, and one draw needn't show every extreme that they name: Partition q sends the first send_count[q, p] entries of send_blocks[q, p] to partition p; send_count[q, q] = 0, and every partition sends 2 blocks to some partition. `tile_row`: 8 marks an unused slot. Slots below 32 take own blocks; slot 32 + q * 2 + c is used only if c < send_count[q, p]. Partition 0 uses all its own-block slots. `tile_src`: slots below 32 name an own block below 8; slot 32 + m names source slot 8 + m.
All inputs are finite; a program needn't handle non-finite values.
Results may differ from a plain program's by a relative error of at most 0.007.
Values may be sent and summed in bfloat16 or wider, within the bound.
A program may use at most 128 MiB of HBM per device.

v0:
```python
import jax
import jax.numpy as jnp
from jax import lax
from jax.sharding import PartitionSpec as P

B = 128
NB = 8
CAP = 2


def receive_blocks(outgoing, peer_count, panel_width):
    arrived = lax.all_to_all(outgoing, "dom", split_axis=0, concat_axis=0, tiled=True)
    return arrived.reshape(peer_count * CAP, B, panel_width)


def shards(
    features, weight, bias, cotangent, tile_vals, tile_row, tile_src, send_blocks, send_count
):
    row_count, panel_width = features.shape
    peer_count = lax.axis_size("dom")
    gathered = lax.all_gather(features, "rep", axis=1, tiled=True)
    hidden = jnp.dot(gathered, weight, preferred_element_type=jnp.float32).astype(jnp.bfloat16)
    hidden_blocks = hidden.reshape(NB, B, panel_width)
    targets = send_blocks[0]
    counts = send_count[0]
    keep_slot = jnp.arange(CAP, dtype=jnp.int32)[None, :] < counts[:, None]
    outgoing = hidden_blocks[targets]
    outgoing = jnp.where(keep_slot[:, :, None, None], outgoing, jnp.zeros_like(outgoing))
    tile_set = tile_vals[0]
    tile_rows = tile_row[0]
    tile_sources = tile_src[0]
    arrived = receive_blocks(outgoing, peer_count, panel_width)
    sources = jnp.concatenate([hidden_blocks, arrived], 0)
    product = jnp.einsum(
        "kab,kbf->kaf", tile_set, sources[tile_sources], preferred_element_type=jnp.float32
    )
    aggregate = jax.ops.segment_sum(product, tile_rows, NB + 1)[:NB]
    shifted = aggregate.reshape(row_count, panel_width) + bias.astype(jnp.float32)
    sigma = jax.nn.sigmoid(shifted)
    out = (shifted * sigma).astype(jnp.bfloat16)
    grad_pre = (cotangent.astype(jnp.float32) * sigma * (1.0 + shifted * (1.0 - sigma))).astype(
        jnp.bfloat16
    )
    pre_padded = jnp.concatenate(
        [grad_pre.reshape(NB, B, panel_width), jnp.zeros((1, B, panel_width), jnp.bfloat16)], 0
    )
    contrib = jnp.einsum(
        "kab,kaf->kbf", tile_set, pre_padded[tile_rows], preferred_element_type=jnp.float32
    )
    per_slot = jax.ops.segment_sum(contrib, tile_sources, NB + peer_count * CAP)
    outbound = per_slot[NB:].reshape(peer_count, CAP, B, panel_width)
    returned = lax.all_to_all(outbound, "dom", split_axis=0, concat_axis=0, tiled=True)
    own_blocks = per_slot[:NB]
    returned = jnp.where(keep_slot[:, :, None, None], returned, jnp.zeros_like(returned))
    grad_blocks = own_blocks + jax.ops.segment_sum(
        returned.reshape(peer_count * CAP, B, panel_width), targets.reshape(-1), NB
    )
    grad_agg = grad_blocks.reshape(row_count, panel_width).astype(jnp.bfloat16)
    weight_part = jnp.dot(gathered.T, grad_agg, preferred_element_type=jnp.float32)
    bias_part = jnp.sum(grad_pre.astype(jnp.float32), 0)
    grad_weight, grad_bias = lax.psum((weight_part, bias_part), "dom")
    partial_terms = jnp.dot(grad_agg, weight.T, preferred_element_type=jnp.float32)
    grad_input = lax.psum_scatter(partial_terms, "rep", scatter_dimension=1, tiled=True).astype(
        jnp.bfloat16
    )
    return (out, grad_input, grad_weight, grad_bias)


def solution(mesh):
    in_specs = (
        P("dom", "rep"),
        P(None, "rep"),
        P("rep"),
        P("dom", "rep"),
        P("dom", None, None, None),
        P("dom", None),
        P("dom", None),
        P("dom", None, None),
        P("dom", None),
    )
    out_specs = (P("dom", "rep"), P("dom", "rep"), P(None, "rep"), P("rep"))
    return jax.shard_map(shards, mesh=mesh, in_specs=in_specs, out_specs=out_specs, check_vma=False)
```

profile of v0, /device:TPU:1, one launch (start us, length us, event | category | flops | bytes accessed | tf_op | source)
XLA Modules:
  0.0 723.8 jit_solution(12466726873163206390)
XLA Ops:
  7.2 0.0 copy-start
  7.2 0.0 all-gather.2.cloned.1.call-start
  7.2 0.7 all-gather.2.cloned.1.call-update
  7.9 0.7 compare_select_fusion.2
  8.6 0.1 copy.18
  8.7 0.1 reshape.145
  8.9 0.7 iota_compare_fusion
  9.6 31.6 %all-gather.2.cloned.1.call-done = bf16[1024,512]{1,0:T(8,128)(2,1)} async-done(((bf16[1024,128]{1,0:T(8,128)(2,1)}), bf16[1024,512]{1,0:T(8,128)(2,1)}) %all-gather.2.cloned.1.call-update) | async-done | bytes 1048592 | tf_op jit(solution)/shard_map/all_gather | solution.py:21
  41.2 0.0 copy-done
  41.2 1.7 convolution_convert_fusion
  42.8 3.0 gather_fusion
  45.9 4.5 broadcast_select_fusion.1
  50.4 11.9 %all-to-all-start = ((bf16[64,2,128,128]{3,2,1,0:T(8,128)(2,1)}), bf16[64,2,128,128]{3,2,1,0:T(8,128)(2,1)}, u32[]{:S(2)}, u32[]{:S(2)}) async-start(bf16[64,2,128,128]{3,2,1,0:T(8,128)(2,1)} %broadcast_select_fusion.1), calls=%async_computation | async-start | bytes 8388608 | tf_op jit(solution)/shard_map/all_to_all | solution.py:12
  62.3 0.0 copy-done.6
  62.3 0.0 copy-done.4
  62.3 0.0 copy-done.3
  62.4 94.3 %all-to-all-done = bf16[64,2,128,128]{3,2,1,0:T(8,128)(2,1)} async-done(((bf16[64,2,128,128]{3,2,1,0:T(8,128)(2,1)}), bf16[64,2,128,128]{3,2,1,0:T(8,128)(2,1)}, u32[]{:S(2)}, u32[]{:S(2)}) %all-to-all-start) | async-done | bytes 4194336 | tf_op jit(solution)/shard_map/all_to_all | solution.py:12
  156.7 4.6 pad_maximum_fusion
  161.3 10.0 %gather_fusion.1 = bf16[160,128,128]{2,1,0:T(8,128)(2,1)} fusion(bf16[136,128,128]{2,1,0:T(8,128)(2,1)} %pad_maximum_fusion, s32[1024]{0:T(1024)S(1)} %pad_clamp_fusion.1), kind=kCustom, calls=%fused_computation.1 | custom fusion | bytes 10486400 | tf_op jit(solution)/shard_map/gather | solution.py:35
  171.3 11.8 %fusion.4 = f32[160,128,128]{1,2,0:T(8,128)} fusion(bf16[160,128,128]{2,1,0:T(8,128)(2,1)} %gather_fusion.1, bf16[1,160,128,128]{3,2,1,0:T(8,128)(2,1)} %param.13), kind=kOutput, calls=%fused_computation.13 | convolution fusion | flops 671088640 | bytes 20971520 | tf_op jit(solution)/shard_map/kab,kbf->kaf/dot_general | solution.py:34
  183.2 11.7 %copy.20 = f32[160,128,128]{2,1,0:T(8,128)} copy(f32[160,128,128]{1,2,0:T(8,128)} %fusion.4) | data formatting | bytes 20971520 | tf_op jit(solution)/shard_map/kab,kbf->kaf/dot_general | solution.py:34
  194.9 0.0 copy-start.2
  194.9 21.1 %scatter_fusion = f32[9,128,128]{2,1,0:T(8,128)S(1)} fusion(f32[9,128,128]{2,1,0:T(8,128)S(1)} %broadcast_in_dim.19, s32[160]{0:T(256)S(1)} %bitcast.58, f32[160,128,128]{2,1,0:T(8,128)} %copy.20), kind=kCustom, calls=%fused_computation.3 | custom fusion | flops 2621440 | bytes 31457920 | tf_op jit(solution)/shard_map/scatter-add | solution.py:37
  216.2 1.0 convert_reduce_fusion
  217.2 7.5 %gather_fusion.2 = bf16[160,128,128]{2,1,0:T(8,128)(2,1)} fusion(bf16[9,128,128]{2,1,0:T(8,128)(2,1)S(1)} %concatenate.7, s32[1024]{0:T(1024)S(1)} %pad_clamp_fusion), kind=kCustom, calls=%fused_computation.2 | custom fusion | bytes 10486400 | tf_op jit(solution)/shard_map/gather | solution.py:48
  224.6 9.8 %fusion.7 = f32[160,128,128]{1,2,0:T(8,128)} fusion(bf16[160,128,128]{2,1,0:T(8,128)(2,1)} %gather_fusion.2, bf16[1,160,128,128]{3,2,1,0:T(8,128)(2,1)} %param.13), kind=kOutput, calls=%fused_computation.14 | convolution fusion | flops 671088640 | bytes 20971520 | tf_op jit(solution)/shard_map/kab,kaf->kbf/dot_general | solution.py:47
  234.4 11.8 %copy.22 = f32[160,128,128]{2,1,0:T(8,128)} copy(f32[160,128,128]{1,2,0:T(8,128)} %fusion.7) | data formatting | bytes 20971520 | tf_op jit(solution)/shard_map/kab,kaf->kbf/dot_general | solution.py:47
  246.2 4.6 broadcast_in_dim.38
  250.8 33.2 %scatter_fusion.1 = f32[136,128,128]{2,1,0:T(8,128)} fusion(f32[136,128,128]{2,1,0:T(8,128)} %broadcast_in_dim.38, s32[160]{0:T(256)S(1)} %bitcast.59, f32[160,128,128]{2,1,0:T(8,128)} %copy.22), kind=kCustom, calls=%fused_computation.4 | custom fusion | flops 2621440 | bytes 31457920 | tf_op jit(solution)/shard_map/scatter-add | solution.py:50
  284.0 7.9 %slice.20 = f32[128,128,128]{2,1,0:T(8,128)} slice(f32[136,128,128]{2,1,0:T(8,128)} %scatter_fusion.1), slice={[8:136], [0:128], [0:128]} | slice | bytes 16777216 | tf_op jit(solution)/shard_map/slice | solution.py:51
  291.8 7.6 %all-to-all-start.1 = ((f32[64,2,128,128]{3,2,1,0:T(8,128)}), f32[64,2,128,128]{3,2,1,0:T(8,128)}, u32[]{:S(2)}, u32[]{:S(2)}) async-start(f32[64,2,128,128]{3,2,1,0:T(8,128)} %bitcast.52), calls=%async_computation.1 | async-start | bytes 16777216 | tf_op jit(solution)/shard_map/all_to_all | solution.py:52
  299.4 0.0 all-reduce.3.cloned.1.call-start
  299.5 0.1 copy.23
  299.6 0.1 reshape.185
  299.7 1.1 slice.19
  300.8 181.5 %all-to-all-done.1 = f32[64,2,128,128]{3,2,1,0:T(8,128)} async-done(((f32[64,2,128,128]{3,2,1,0:T(8,128)}), f32[64,2,128,128]{3,2,1,0:T(8,128)}, u32[]{:S(2)}, u32[]{:S(2)}) %all-to-all-start.1) | async-done | bytes 8388640 | tf_op jit(solution)/shard_map/all_to_all | solution.py:52
  482.3 7.2 broadcast_select_fusion
  489.6 17.0 %scatter_fusion.2 = f32[8,128,128]{2,1,0:T(8,128)S(1)} fusion(f32[8,128,128]{2,1,0:T(8,128)S(1)} %slice.19, s32[128]{0:T(128)S(1)} %reshape.185, f32[128,128,128]{2,1,0:T(8,128)} %bitcast.53), kind=kCustom, calls=%fused_computation.5 | custom fusion | flops 2097152 | bytes 25166336 | tf_op jit(solution)/shard_map/scatter-add | solution.py:55
  506.6 1.0 convolution_bitcast_fusion
  507.7 0.0 all-reduce.3.cloned.1.call-update
  507.7 0.0 reduce-scatter.2.cloned.1.call-start
  507.7 1.8 fusion.10
  509.5 0.0 reduce-scatter.2.cloned.1.call-update
  509.6 127.7 %psum.15 = f32[128]{0:T(128)} all-reduce(f32[128]{0:T(128)S(1)} %get-tuple-element.12), channel_id=1, replica_groups=mesh['dom'=64,'rep'=4] {'dom'}, use_global_device_ids=true, to_apply=%region_6.7 | all-reduce | flops 128 | bytes 1024 | tf_op jit(solution)/shard_map/psum | solution.py:61
  637.3 46.1 %all-reduce.3.cloned.1.call-done = f32[512,128]{0,1:T(8,128)} async-done(((f32[512,128]{0,1:T(8,128)}), f32[512,128]{0,1:T(8,128)}) %all-reduce.3.cloned.1.call-update) | async-done | bytes 262160 | tf_op jit(solution)/shard_map/psum | solution.py:61
  683.4 1.8 copy.24
  685.1 30.4 %reduce-scatter.2.cloned.1.call-done = f32[1024,128]{1,0:T(8,128)} async-done(((f32[1024,512]{1,0:T(8,128)}), f32[1024,128]{1,0:T(8,128)}) %reduce-scatter.2.cloned.1.call-update) | async-done | bytes 524304 | tf_op jit(solution)/shard_map/reduce_scatter | solution.py:63
  715.5 1.8 convert_element_type.34
  (18 shorter events, 0.2 us)
Async XLA Ops:
  7.2 34.0 %copy-start = (bf16[512,128]{1,0:T(8,128)(2,1)S(1)}, bf16[512,128]{1,0:T(8,128)(2,1)}, u32[]{:S(2)}) copy-start(bf16[512,128]{1,0:T(8,128)(2,1)} %param.10) | copy-start | bytes 393220
  7.2 34.0 %all-gather.2.cloned.1.call-start = ((), (), s32[]{:S(2)}) async-start(), calls=%async_computation.3 | async-start | bytes 1310720 | tf_op jit(solution)/shard_map/all_gather | solution.py:21
  50.4 11.9 %copy-start.6 = (bf16[128]{0:T(256)(128)(2,1)S(1)}, bf16[128]{0:T(256)(128)(2,1)}, u32[]{:S(2)}) copy-start(bf16[128]{0:T(256)(128)(2,1)} %param.11) | copy-start | bytes 772
  50.4 11.9 %copy-start.4 = (s32[1,160]{1,0:T(1,128)S(1)}, s32[1,160]{1,0:T(1,128)}, u32[]{:S(2)}) copy-start(s32[1,160]{1,0:T(1,128)} %param.15) | copy-start | bytes 1924
  50.4 12.0 %copy-start.3 = (s32[1,160]{1,0:T(1,128)S(1)}, s32[1,160]{1,0:T(1,128)}, u32[]{:S(2)}) copy-start(s32[1,160]{1,0:T(1,128)} %param.14) | copy-start | bytes 1924
  50.4 106.3 %all-to-all-start = ((bf16[64,2,128,128]{3,2,1,0:T(8,128)(2,1)}), bf16[64,2,128,128]{3,2,1,0:T(8,128)(2,1)}, u32[]{:S(2)}, u32[]{:S(2)}) async-start(bf16[64,2,128,128]{3,2,1,0:T(8,128)(2,1)} %broadcast_select_fusion.1), calls=%async_computation | async-start | bytes 8388608 | tf_op jit(solution)/shard_map/all_to_all | solution.py:12
  194.9 21.2 %copy-start.2 = (bf16[1024,128]{1,0:T(8,128)(2,1)S(1)}, bf16[1024,128]{1,0:T(8,128)(2,1)}, u32[]{:S(2)}) copy-start(bf16[1024,128]{1,0:T(8,128)(2,1)} %param.12) | copy-start | bytes 786436
  291.8 7.7 %copy-start.5 = (s32[1,64,2]{1,2,0:T(2,128)S(1)}, s32[1,64,2]{1,2,0:T(2,128)}, u32[]{:S(2)}) copy-start(s32[1,64,2]{1,2,0:T(2,128)} %param.16) | copy-start | bytes 1540
  291.8 190.5 %all-to-all-start.1 = ((f32[64,2,128,128]{3,2,1,0:T(8,128)}), f32[64,2,128,128]{3,2,1,0:T(8,128)}, u32[]{:S(2)}, u32[]{:S(2)}) async-start(f32[64,2,128,128]{3,2,1,0:T(8,128)} %bitcast.52), calls=%async_computation.1 | async-start | bytes 16777216 | tf_op jit(solution)/shard_map/all_to_all | solution.py:52
  299.4 383.9 %all-reduce.3.cloned.1.call-start = ((), (), s32[]{:S(2)}) async-start(), calls=%async_computation.5 | async-start | bytes 524288 | tf_op jit(solution)/shard_map/psum | solution.py:61
  489.5 17.1 %copy-start.1 = (bf16[1024,512]{1,0:T(8,128)(2,1)S(1)}, bf16[1024,512]{1,0:T(8,128)(2,1)}, u32[]{:S(2)}) copy-start(bf16[1024,512]{1,0:T(8,128)(2,1)} %all-gather.2.cloned.1.call-done) | copy-start | bytes 3145732
  507.7 207.8 %reduce-scatter.2.cloned.1.call-start = ((), (), s32[]{:S(2)}) async-start(), calls=%async_computation.4 | async-start | bytes 2621440 | tf_op jit(solution)/shard_map/reduce_scatter | solution.py:63
Sparse Core Ops, SparseCore 0:
  9.8 31.3 all-gather.1
  507.8 175.4 all-reduce.2
  686.1 29.4 reduce-scatter.1
where the time goes:
time: 726 us; the launch traced here: 724 us
  waiting for transfers between devices  385 us (53%)
  blocking collectives  128 us (18%)
  other arithmetic  91.9 us (13%)
  local copies, waits for them, and re-layouts  60 us (8%)
  matrix products  26.1 us (4%)
  starting transfers between devices  19.6 us (3%)
  between operations  13.9 us (2%)
    all_to_all x1, waiting for transfers between devices, shards(): lax.all_to_all(outbound, 'dom', split_axis=0, concat_axis=0, tiled=True)  182 us
    psum x1, blocking collectives, shards(): grad_weight, grad_bias = lax.psum((weight_part, bias_part), 'dom')  128 us
    all_to_all x1, waiting for transfers between devices, receive_blocks(): lax.all_to_all(outgoing, 'dom', split_axis=0, concat_axis=0, tiled=True)  94.3 us
    psum x1, waiting for transfers between devices, shards(): grad_weight, grad_bias = lax.psum((weight_part, bias_part), 'dom')  46.1 us
    scatter-add x1, other arithmetic, shards(): per_slot = jax.ops.segment_sum(contrib, tile_sources, NB + peer_count * CAP)  33.2 us
    all_gather x1, waiting for transfers between devices, shards(): gathered = lax.all_gather(features, 'rep', axis=1, tiled=True)  31.6 us
    reduce_scatter x1, waiting for transfers between devices, shards(): lax.psum_scatter(partial_terms, 'rep', scatter_dimension=1, tiled=True)  30.4 us
    scatter-add x1, other arithmetic, shards(): aggregate = jax.ops.segment_sum(product, tile_rows, NB + 1)[:NB]  21.1 us
  transfers between devices with their start and end apart: 5, of which 5 were waited for; matrix products, arithmetic and copies ran while one was open for 1% of the time, Pallas kernels for 0%

commit v1 on v0

--- a/solution.py
+++ b/solution.py
@@ -6,6 +6,17 @@
 B = 128
 NB = 8
 CAP = 2
+
+
+def pass_along(x, axis, along):
+    peers = lax.axis_size(axis)
+    right = [(i, (i + 1) % peers) for i in range(peers)]
+    parts = [x]
+    for hop in range(1, peers):
+        parts = [lax.ppermute(parts[0], axis, right), *parts]
+    full = jnp.concatenate(parts, axis=along)
+    shift = (lax.axis_index(axis) + 1) * parts[-1].shape[along]
+    return jnp.roll(full, shift, axis=along)
 
 
 def receive_blocks(outgoing, peer_count, panel_width):
@@ -18,7 +29,7 @@
 ):
     row_count, panel_width = features.shape
     peer_count = lax.axis_size("dom")
-    gathered = lax.all_gather(features, "rep", axis=1, tiled=True)
+    gathered = pass_along(features, "rep", 1)
     hidden = jnp.dot(gathered, weight, preferred_element_type=jnp.float32).astype(jnp.bfloat16)
     hidden_blocks = hidden.reshape(NB, B, panel_width)
     targets = send_blocks[0]

time: 726 us -> 693 us (0.955)
  waiting for transfers between devices: 385 us -> 337 us
  starting transfers between devices: 19.6 us -> 30.4 us
    all_gather x1 -> x0, waiting for transfers between devices: 31.6 us -> none  [shards(): gathered = lax.all_gather(features, 'rep', axis=1, tiled=True)]
    reduce_scatter x1, waiting for transfers between devices: 30.4 us -> 0.01 us  [shards(): lax.psum_scatter(partial_terms, 'rep', scatter_dimension=1, tiled=True)]
    ppermute x0 -> x3, waiting for transfers between devices: none -> 14 us  [pass_along(): parts = [lax.ppermute(parts[0], axis, right), *parts]]
  transfers between devices with their start and end apart: 5 -> 7, of which waited for: 5 -> 6; matrix products, arithmetic and copies ran while one was open for 1% -> 1% of each run, Pallas kernels for 0% -> 0%
where the time goes in v1:
time: 693 us; the launch traced here: 691 us
  waiting for transfers between devices  337 us (49%)
  blocking collectives  128 us (18%)
  other arithmetic  92.6 us (13%)
  local copies, waits for them, and re-layouts  62.4 us (9%)
  starting transfers between devices  30.4 us (4%)
  matrix products  25 us (4%)
  between operations  15.7 us (2%)
    all_to_all x1, waiting for transfers between devices, shards(): lax.all_to_all(outbound, 'dom', split_axis=0, concat_axis=0, tiled=True)  182 us
    psum x1, blocking collectives, shards(): grad_weight, grad_bias = lax.psum((weight_part, bias_part), 'dom')  128 us
    all_to_all x1, waiting for transfers between devices, receive_blocks(): lax.all_to_all(outgoing, 'dom', split_axis=0, concat_axis=0, tiled=True)  94.3 us
    psum x1, waiting for transfers between devices, shards(): grad_weight, grad_bias = lax.psum((weight_part, bias_part), 'dom')  47.5 us
    scatter-add x1, other arithmetic, shards(): per_slot = jax.ops.segment_sum(contrib, tile_sources, NB + peer_count * CAP)  33.2 us
    scatter-add x1, other arithmetic, shards(): aggregate = jax.ops.segment_sum(product, tile_rows, NB + 1)[:NB]  21.1 us
    all_to_all x1, starting transfers between devices, receive_blocks(): lax.all_to_all(outgoing, 'dom', split_axis=0, concat_axis=0, tiled=True)  18 us
    scatter-add x1, other arithmetic, shards(): jax.ops.segment_sum(returned.reshape(peer_count * CAP, B, panel_width), t...  17 us
  transfers between devices with their start and end apart: 7, of which 6 were waited for; matrix products, arithmetic and copies ran while one was open for 1% of the time, Pallas kernels for 0%

profile of v1, /device:TPU:1, one launch (start us, length us, event | category | flops | bytes accessed | tf_op | source)
XLA Modules:
  0.0 691.3 jit_solution(8917627142043339561)
XLA Ops:
  8.0 2.1 collective-permute-start
  10.1 5.2 collective-permute-done
  15.4 1.9 collective-permute-start.1
  17.2 0.7 compare_select_fusion.2
  17.9 0.1 copy.17
  18.0 0.1 reshape.145
  18.2 0.7 compare_select_fusion
  18.8 3.7 collective-permute-done.1
  22.5 0.7 collective-permute-start.2
  23.2 0.7 iota_compare_fusion
  23.9 5.0 collective-permute-done.2
  29.0 0.1 constant_dynamic-update-slice_fusion.6
  29.1 0.1 constant_dynamic-update-slice_fusion.5
  29.2 1.0 constant_dynamic-update-slice_fusion.4
  30.3 0.1 constant_dynamic-update-slice_fusion.3
  30.4 0.1 constant_dynamic-update-slice_fusion.2
  30.5 0.1 constant_dynamic-update-slice_fusion.1
  30.6 1.0 constant_dynamic-update-slice_fusion
  31.6 0.4 convolution_convert_fusion
  32.1 3.0 gather_fusion
  35.1 4.5 broadcast_select_fusion.1
  39.6 18.0 %all-to-all-start = ((bf16[64,2,128,128]{3,2,1,0:T(8,128)(2,1)}), bf16[64,2,128,128]{3,2,1,0:T(8,128)(2,1)}, u32[]{:S(2)}, u32[]{:S(2)}) async-start(bf16[64,2,128,128]{3,2,1,0:T(8,128)(2,1)} %broadcast_select_fusion.1), calls=%async_computation | async-start | bytes 8388608 | tf_op jit(solution)/shard_map/all_to_all | solution.py:23
  57.7 94.3 %all-to-all-done = bf16[64,2,128,128]{3,2,1,0:T(8,128)(2,1)} async-done(((bf16[64,2,128,128]{3,2,1,0:T(8,128)(2,1)}), bf16[64,2,128,128]{3,2,1,0:T(8,128)(2,1)}, u32[]{:S(2)}, u32[]{:S(2)}) %all-to-all-start) | async-done | bytes 4194336 | tf_op jit(solution)/shard_map/all_to_all | solution.py:23
  152.0 4.6 pad_maximum_fusion
  156.7 10.0 %gather_fusion.1 = bf16[160,128,128]{2,1,0:T(8,128)(2,1)} fusion(bf16[136,128,128]{2,1,0:T(8,128)(2,1)} %pad_maximum_fusion, s32[1024]{0:T(1024)S(1)} %pad_clamp_fusion.1), kind=kCustom, calls=%fused_computation.1 | custom fusion | bytes 10486400 | tf_op jit(solution)/shard_map/gather | solution.py:46
  166.7 11.8 %fusion.4 = f32[160,128,128]{1,2,0:T(8,128)} fusion(bf16[160,128,128]{2,1,0:T(8,128)(2,1)} %gather_fusion.1, bf16[1,160,128,128]{3,2,1,0:T(8,128)(2,1)} %param.13), kind=kOutput, calls=%fused_computation.13 | convolution fusion | flops 671088640 | bytes 20971520 | tf_op jit(solution)/shard_map/kab,kbf->kaf/dot_general | solution.py:45
  178.5 11.7 %copy.19 = f32[160,128,128]{2,1,0:T(8,128)} copy(f32[160,128,128]{1,2,0:T(8,128)} %fusion.4) | data formatting | bytes 20971520 | tf_op jit(solution)/shard_map/kab,kbf->kaf/dot_general | solution.py:45
  190.3 21.1 %scatter_fusion = f32[9,128,128]{2,1,0:T(8,128)S(1)} fusion(f32[9,128,128]{2,1,0:T(8,128)S(1)} %broadcast_in_dim.19, s32[160]{0:T(256)S(1)} %bitcast.54, f32[160,128,128]{2,1,0:T(8,128)} %copy.19), kind=kCustom, calls=%fused_computation.3 | custom fusion | flops 2621440 | bytes 31457920 | tf_op jit(solution)/shard_map/scatter-add | solution.py:48
  211.5 1.0 convert_reduce_fusion
  212.5 7.5 %gather_fusion.2 = bf16[160,128,128]{2,1,0:T(8,128)(2,1)} fusion(bf16[9,128,128]{2,1,0:T(8,128)(2,1)S(1)} %concatenate.14, s32[1024]{0:T(1024)S(1)} %get-tuple-element.7), kind=kCustom, calls=%fused_computation.2 | custom fusion | bytes 10486400 | tf_op jit(solution)/shard_map/gather | solution.py:59
  220.0 9.8 %fusion.7 = f32[160,128,128]{1,2,0:T(8,128)} fusion(bf16[160,128,128]{2,1,0:T(8,128)(2,1)} %gather_fusion.2, bf16[1,160,128,128]{3,2,1,0:T(8,128)(2,1)} %param.13), kind=kOutput, calls=%fused_computation.14 | convolution fusion | flops 671088640 | bytes 20971520 | tf_op jit(solution)/shard_map/kab,kaf->kbf/dot_general | solution.py:58
  229.8 11.8 %copy.21 = f32[160,128,128]{2,1,0:T(8,128)} copy(f32[160,128,128]{1,2,0:T(8,128)} %fusion.7) | data formatting | bytes 20971520 | tf_op jit(solution)/shard_map/kab,kaf->kbf/dot_general | solution.py:58
  241.6 4.6 broadcast_in_dim.38
  246.1 33.2 %scatter_fusion.1 = f32[136,128,128]{2,1,0:T(8,128)} fusion(f32[136,128,128]{2,1,0:T(8,128)} %broadcast_in_dim.38, s32[160]{0:T(256)S(1)} %bitcast.55, f32[160,128,128]{2,1,0:T(8,128)} %copy.21), kind=kCustom, calls=%fused_computation.4 | custom fusion | flops 2621440 | bytes 31457920 | tf_op jit(solution)/shard_map/scatter-add | solution.py:61
  279.3 7.9 %slice.20 = f32[128,128,128]{2,1,0:T(8,128)} slice(f32[136,128,128]{2,1,0:T(8,128)} %scatter_fusion.1), slice={[8:136], [0:128], [0:128]} | slice | bytes 16777216 | tf_op jit(solution)/shard_map/slice | solution.py:62
  287.2 7.6 %all-to-all-start.1 = ((f32[64,2,128,128]{3,2,1,0:T(8,128)}), f32[64,2,128,128]{3,2,1,0:T(8,128)}, u32[]{:S(2)}, u32[]{:S(2)}) async-start(f32[64,2,128,128]{3,2,1,0:T(8,128)} %bitcast.48), calls=%async_computation.1 | async-start | bytes 16777216 | tf_op jit(solution)/shard_map/all_to_all | solution.py:63
  294.9 0.1 copy.22
  295.0 0.1 reshape.185
  295.1 1.1 slice.19
  296.2 181.5 %all-to-all-done.1 = f32[64,2,128,128]{3,2,1,0:T(8,128)} async-done(((f32[64,2,128,128]{3,2,1,0:T(8,128)}), f32[64,2,128,128]{3,2,1,0:T(8,128)}, u32[]{:S(2)}, u32[]{:S(2)}) %all-to-all-start.1) | async-done | bytes 8388640 | tf_op jit(solution)/shard_map/all_to_all | solution.py:63
  477.7 7.2 %broadcast_select_fusion = f32[64,2,128,128]{3,2,1,0:T(8,128)} fusion(f32[64,2,128,128]{3,2,1,0:T(8,128)} %all-to-all-done.1, pred[64,2]{1,0:T(8,128)(4,1)S(1)} %iota_compare_fusion), kind=kLoop, calls=%fused_computation.11 | loop fusion | flops 2097152 | bytes 16777344 | tf_op jit(solution)/shard_map/jit(_where)/select_n | solution.py:65
  484.9 17.0 %scatter_fusion.2 = f32[8,128,128]{2,1,0:T(8,128)S(1)} fusion(f32[8,128,128]{2,1,0:T(8,128)S(1)} %slice.19, s32[128]{0:T(128)S(1)} %reshape.185, f32[128,128,128]{2,1,0:T(8,128)} %bitcast.49), kind=kCustom, calls=%fused_computation.5 | custom fusion | flops 2097152 | bytes 25166336 | tf_op jit(solution)/shard_map/scatter-add | solution.py:66
  502.0 1.8 fusion.15
  503.9 1.2 fusion.10
  505.1 127.8 %psum.15 = f32[128]{0:T(128)} all-reduce(f32[128]{0:T(128)S(1)} %get-tuple-element.4), channel_id=1, replica_groups=mesh['dom'=64,'rep'=4] {'dom'}, use_global_device_ids=true, to_apply=%region_6.7 | all-reduce | flops 128 | bytes 1024 | tf_op jit(solution)/shard_map/psum | solution.py:72
  632.9 1.8 convert_element_type.34
  634.6 47.5 %all-reduce.3.cloned.1.call-done = f32[512,128]{1,0:T(8,128)} async-done(((f32[512,128]{1,0:T(8,128)}), f32[512,128]{1,0:T(8,128)}) %all-reduce.3.cloned.1.call-update) | async-done | bytes 262160 | tf_op jit(solution)/shard_map/psum | solution.py:72
  682.1 1.7 copy.36
  (26 shorter events, 0.4 us)
Async XLA Ops:
  8.0 23.6 %copy-start = (bf16[512,128]{1,0:T(8,128)(2,1)S(1)}, bf16[512,128]{1,0:T(8,128)(2,1)}, u32[]{:S(2)}) copy-start(bf16[512,128]{1,0:T(8,128)(2,1)} %param.10) | copy-start | bytes 393220
  8.0 7.4 %collective-permute-start = (bf16[1024,128]{1,0:T(8,128)(2,1)}, bf16[1024,128]{1,0:T(8,128)(2,1)S(1)}, u32[]{:S(2)}, u32[]{:S(2)}) collective-permute-start(bf16[1024,128]{1,0:T(8,128)(2,1)} %param.9), channel_id=1, source_target_pairs={{0,1},{1,2},{2,3},{3,0},{4,5},{5,6},{6,7},{7,4},{8,9},{9,10},{10,1... | collective-permute-start | bytes 786440 | tf_op jit(solution)/shard_map/ppermute | solution.py:16
  15.4 7.2 %collective-permute-start.1 = (bf16[1024,128]{1,0:T(8,128)(2,1)S(1)}, bf16[1024,128]{1,0:T(8,128)(2,1)S(1)}, u32[]{:S(2)}, u32[]{:S(2)}) collective-permute-start(bf16[1024,128]{1,0:T(8,128)(2,1)S(1)} %collective-permute-done), channel_id=1, source_target_pairs={{0,1},{1,2},{2,3},{3,0},{4,5},{5,6},{6,7},{7,4},{8,9},{9,10},{10,1... | collective-permute-start | bytes 786440 | tf_op jit(solution)/shard_map/ppermute | solution.py:16
  22.5 6.4 collective-permute-start.2
  39.6 18.1 %copy-start.5 = (bf16[128]{0:T(256)(128)(2,1)S(1)}, bf16[128]{0:T(256)(128)(2,1)}, u32[]{:S(2)}) copy-start(bf16[128]{0:T(256)(128)(2,1)} %param.11) | copy-start | bytes 772
  39.6 18.1 %copy-start.3 = (s32[1,160]{1,0:T(1,128)S(1)}, s32[1,160]{1,0:T(1,128)}, u32[]{:S(2)}) copy-start(s32[1,160]{1,0:T(1,128)} %param.15) | copy-start | bytes 1924
  39.6 112.4 %all-to-all-start = ((bf16[64,2,128,128]{3,2,1,0:T(8,128)(2,1)}), bf16[64,2,128,128]{3,2,1,0:T(8,128)(2,1)}, u32[]{:S(2)}, u32[]{:S(2)}) async-start(bf16[64,2,128,128]{3,2,1,0:T(8,128)(2,1)} %broadcast_select_fusion.1), calls=%async_computation | async-start | bytes 8388608 | tf_op jit(solution)/shard_map/all_to_all | solution.py:23
  178.5 11.8 %copy-start.2 = (s32[1,160]{1,0:T(1,128)S(1)}, s32[1,160]{1,0:T(1,128)}, u32[]{:S(2)}) copy-start(s32[1,160]{1,0:T(1,128)} %param.14) | copy-start | bytes 1924
  190.3 21.2 %copy-start.1 = (bf16[1024,128]{1,0:T(8,128)(2,1)S(1)}, bf16[1024,128]{1,0:T(8,128)(2,1)}, u32[]{:S(2)}) copy-start(bf16[1024,128]{1,0:T(8,128)(2,1)} %param.12) | copy-start | bytes 786436
  287.2 7.7 %copy-start.4 = (s32[1,64,2]{1,2,0:T(2,128)S(1)}, s32[1,64,2]{1,2,0:T(2,128)}, u32[]{:S(2)}) copy-start(s32[1,64,2]{1,2,0:T(2,128)} %param.16) | copy-start | bytes 1540
  287.2 190.5 %all-to-all-start.1 = ((f32[64,2,128,128]{3,2,1,0:T(8,128)}), f32[64,2,128,128]{3,2,1,0:T(8,128)}, u32[]{:S(2)}, u32[]{:S(2)}) async-start(f32[64,2,128,128]{3,2,1,0:T(8,128)} %bitcast.48), calls=%async_computation.1 | async-start | bytes 16777216 | tf_op jit(solution)/shard_map/all_to_all | solution.py:63
  294.8 338.0 %reduce-scatter.2.cloned.1.call-start = ((), (), s32[]{:S(2)}) async-start(), calls=%async_computation.3 | async-start | bytes 2621440 | tf_op jit(solution)/shard_map/reduce_scatter | solution.py:74
  503.8 178.3 %all-reduce.3.cloned.1.call-start = ((), (), s32[]{:S(2)}) async-start(), calls=%async_computation.4 | async-start | bytes 524288 | tf_op jit(solution)/shard_map/psum | solution.py:72
Sparse Core Ops, SparseCore 0:
  503.9 30.1 reduce-scatter.1
Sparse Core Ops, SparseCore 1:
  508.8 173.3 all-reduce.2
